TPU v7x, 32 devices: a whole 2x2x4 slice. The times are simulated.
32 devices in a mesh: groups: 2 (over y), ctx: 4 (over z), chan: 4 (over x, core).
Axes of the slice: x: 2, y: 2, z: 4, core: 2. Of those that a mesh axis runs over, the one named last changes fastest.
Arguments:
- q_feat: bfloat16 [4096, 8192], P(('groups', 'ctx'), 'chan'), parts along dimension 0, may hold values from -6 to 6
- k_feat: bfloat16 [4096, 8192], P(('groups', 'ctx'), 'chan'), parts along dimension 0, may hold values from -6 to 6
- v_feat: bfloat16 [4096, 8192], P(('groups', 'ctx'), 'chan'), parts along dimension 0, may hold values from -6 to 6
- pole_rate: float32 [16, 8192], P(None, 'chan'), may hold values from 4.8828126e-05 to 0.03
- residue: float32 [16, 8192], P(None, 'chan'), may hold values from -1.5 to 1.5
- skip_gain: float32 [8192], P('chan'), may hold values from 0.5 to 1.5
- lengths: int32 [8], P('groups'), parts along dimension 0, may hold values from 1 to 1024, 2048 in all
- owners: int32 [8], P('groups'), parts along dimension 0, may hold values from 0 to 3, as said below
Outputs:
- mixed_out: bfloat16 [4096, 8192], P(('groups', 'ctx'), 'chan'), parts along dimension 0
- decode_state: float32 [8, 16, 8192], P(('groups', 'ctx'), None, 'chan'), parts along dimension 0
There are 2 independent parts, one for each index of `groups`. A program takes and returns all parts, laid end to end along the dimension named above; an argument that names none is the same for every part. Nothing has to cross between parts.
Inputs may be any that keep to these rules, and one draw needn't show every extreme that they name: The 4 lengths sum to 2048; the longest is exactly 1024. The 4 owners are distinct.
All inputs are finite; a program needn't handle non-finite values.
Results may differ from a plain program's by a relative error of at most 0.001.
Values sent between devices are 32-bit elements; how exact they have to be, the bound alone decides.
No kernel may reach another device: no remote copies, remote signals or barrier semaphores. Data moves between devices by JAX's collectives and lax.ppermute only.
A program may use at most 128 MiB of HBM per device.

v0:
```python
import functools

import jax
import jax.numpy as jnp
from jax import lax
from jax.experimental import pallas as pl
from jax.experimental.pallas import tpu as pltpu
from jax.sharding import PartitionSpec as P

LANES = 128
SUBS = 8
PACKED = 16
LOAD = 256
CHUNK = 128
BLOCK = 16
UNROLL = 8
VMEM_BYTES = 28 * 1024 * 1024
F32 = jnp.float32


def request_span(lengths_ref, request, request_count):
    start = jnp.int32(0)
    length = jnp.int32(0)
    for r in range(request_count):
        start = start + jnp.where(r < request, lengths_ref[r], 0)
        length = length + jnp.where(r == request, lengths_ref[r], 0)
    return start, start + length - 1


def request_at(lengths_ref, position, request_count):
    index = jnp.int32(-1)
    start = jnp.int32(0)
    for r in range(request_count):
        index = index + (start <= position).astype(jnp.int32)
        start = start + lengths_ref[r]
    return index


def request_before(lengths_ref, tok_dev, hop):
    first = lax.axis_index("ctx") * tok_dev
    return request_at(lengths_ref, first - (hop - 1) * tok_dev - 1, lengths_ref.shape[0])


def token_loop(lo, hi, step, carry):
    count = jnp.maximum(hi - lo, 0)
    groups = lax.shift_right_logical(count, jnp.int32(UNROLL.bit_length() - 1))

    def many(g, carry):
        base = lo + g * UNROLL
        for s in range(UNROLL):
            carry = step(base + s, carry)
        return carry

    carry = lax.fori_loop(0, groups, many, carry)
    return lax.fori_loop(lo + groups * UNROLL, lo + count, step, carry)


def half_span(channels):
    tiles = channels // LANES
    return min(tiles, SUBS), max(tiles // SUBS, 1)


def state_rows(p, h, halves):
    return pl.ds(pl.multiple_of((p * halves + h) * SUBS, SUBS), SUBS)


def natural_rows(p, tile, halves):
    return pl.ds((p * halves + tile // SUBS) * SUBS + tile % SUBS, SUBS, stride=halves * SUBS)


def token_rows(t):
    return pl.ds(
        lax.shift_right_logical(t, jnp.int32(3)) * (SUBS * SUBS) + lax.bitwise_and(t, jnp.int32(7)),
        SUBS,
        stride=SUBS,
    )


def block_token(b, s):
    return pl.ds(b * (BLOCK * SUBS) + s // SUBS * (SUBS * SUBS) + s % SUBS, SUBS, stride=SUBS)


def saved_rows(b, p, pole_count):
    return pl.ds(pl.multiple_of((b * pole_count + p) * SUBS, SUBS), SUBS)


def block_parts(lo, hi):
    head = jnp.minimum(hi, lax.bitwise_and(lo + (BLOCK - 1), jnp.int32(-BLOCK)))
    shift = jnp.int32(BLOCK.bit_length() - 1)
    first = lax.shift_right_logical(head + (BLOCK - 1), shift)
    last = jnp.maximum(lax.shift_right_logical(hi, shift), first)
    return head, first, last, jnp.maximum(last * BLOCK, head)


def tile_rows(group, j):
    return pl.ds(pl.multiple_of((group * SUBS + j) * SUBS, SUBS), SUBS)


def each_tile(value_ref):
    pole_count, channels = value_ref.shape
    for p in range(0, pole_count, SUBS):
        for tile in range(channels // LANES):
            yield p, tile, (slice(p, p + SUBS), slice(tile * LANES, (tile + 1) * LANES))


def to_states(ref, states, change):
    _, halves = half_span(ref.shape[1])
    for p, tile, at in each_tile(ref):
        states[natural_rows(p, tile, halves), :] = change(at)


def scaled(rate_ref, residue_ref, at):
    return residue_ref[at] * jnp.sqrt(1.0 - jnp.exp(-2.0 * rate_ref[at]))


def chunk_copy(src, src_at, dst, dst_at, sem, start):
    copy = pltpu.make_async_copy(src.at[src_at], dst.at[dst_at], sem)
    if start:
        copy.start()
    else:
        copy.wait()


def token_chunk(c, size=CHUNK):
    return pl.ds(pl.multiple_of(c * size, size), size)


def fill_rows(k_buf, v_buf, u_rows, c, first_tile, width):
    def block(b, _):
        rows = pl.ds(pl.multiple_of(c * LOAD + b * PACKED, PACKED), PACKED)
        for j in range(width):
            lanes = slice((first_tile + j) * LANES, (first_tile + j + 1) * LANES)
            u = k_buf[rows, lanes].astype(F32) * v_buf[rows, lanes].astype(F32)
            for part in range(PACKED // SUBS):
                group = c * (LOAD // SUBS) + b * (PACKED // SUBS) + part
                u_rows[tile_rows(group, j), :] = u[part * SUBS : (part + 1) * SUBS]
        return 0

    lax.fori_loop(0, LOAD // PACKED, block, 0)


def fill_lengths(bounds_ref, lengths_ref):
    for r in range(bounds_ref.shape[0]):
        lengths_ref[r] = jnp.max(bounds_ref[r]).astype(jnp.int32)


def each_request(lengths_ref, base, extent, body):
    def request(r, start):
        length = lengths_ref[r]
        lo = jnp.maximum(start - base, 0)
        hi = jnp.minimum(start + length - base, extent)

        @pl.when(hi > lo)
        def _():
            body(r, start, lo, hi)

        return start + length

    lax.fori_loop(0, lengths_ref.shape[0], request, jnp.int32(0))


def total(terms):
    while len(terms) > 1:
        terms = [x + y for x, y in zip(terms[::2], terms[1::2])] + terms[len(terms) // 2 * 2 :]
    return terms[0]


def pieces_kernel(
    lengths_hbm, owners_hbm, k_hbm, v_hbm, rate_hbm, residue_hbm,
    cross_ref, near_ref, pair_ref, own_ref, mine_ref, bounds_ref, u_rows, decays, gains, saved,
    k_buf, v_buf, rate_ref, residue_ref, lengths_ref, owners_ref, states, sems, small_sems,
):
    n = lax.axis_size("ctx")
    i = lax.axis_index("ctx")
    request_count = lengths_ref.shape[0]
    pole_count, channels = rate_ref.shape
    tok_dev = k_buf.shape[0]
    width, halves = half_span(channels)
    chunks = tok_dev // LOAD
    first = i * tok_dev
    last = first + tok_dev - 1

    def moves(c, start):
        rows = (token_chunk(c, LOAD), slice(None))
        chunk_copy(k_hbm, rows, k_buf, rows, sems.at[0, c], start)
        chunk_copy(v_hbm, rows, v_buf, rows, sems.at[1, c], start)

    small = [
        pltpu.make_async_copy(src, dst, small_sems.at[n])
        for n, (src, dst) in enumerate(
            (
                (lengths_hbm, lengths_ref),
                (owners_hbm, owners_ref),
                (rate_hbm, rate_ref),
                (residue_hbm, residue_ref),
            )
        )
    ]
    for copy in small:
        copy.start()
    for c in range(chunks):
        moves(c, True)

    def clear(b, _):
        states[pl.ds(pl.multiple_of(b * SUBS, SUBS), SUBS), :] = jnp.zeros((SUBS, LANES), F32)
        return 0

    lax.fori_loop(0, request_count * pole_count * halves, clear, 0)
    for copy in small:
        copy.wait()
    for r in range(request_count):
        bounds_ref[r] = jnp.full((SUBS, LANES), lengths_ref[r].astype(F32), F32)
    to_states(rate_ref, decays, lambda at: jnp.exp(-rate_ref[at]))
    to_states(rate_ref, gains, lambda at: scaled(rate_ref, residue_ref, at))

    def chunk(c, _):
        moves(c, False)
        for h in range(halves):
            fill_rows(k_buf, v_buf, u_rows.at[h], c, h * SUBS, width)
        base = c * LOAD

        def request(r, start, lo, hi):
            head, begin, end, tail = block_parts(base + lo, base + hi)

            def half(h, _):
                decay = [decays[state_rows(p, h, halves), :] for p in range(pole_count)]
                row = r * pole_count
                state = tuple(
                    states[state_rows(row + p, h, halves), :] for p in range(pole_count)
                )

                def advance(state, u):
                    return tuple(s * a + u for s, a in zip(state, decay))

                def single(t, state):
                    return advance(state, u_rows[h, token_rows(t), :])

                def save(b, state):
                    for p in range(pole_count):
                        saved[h, saved_rows(b, p, pole_count), :] = state[p]

                def block(b, state):
                    save(b, state)
                    for s in range(BLOCK):
                        state = advance(state, u_rows[h, block_token(b, s), :])
                    return state

                state = lax.fori_loop(base + lo, head, single, state)
                state = lax.fori_loop(begin, end, block, state)

                @pl.when(base + hi > tail)
                def _():
                    save(end, state)

                state = lax.fori_loop(tail, base + hi, single, state)
                for p in range(pole_count):
                    states[state_rows(row + p, h, halves), :] = state[p]
                return 0

            lax.fori_loop(0, halves, half, 0)

        each_request(lengths_ref, first + base, LOAD, request)
        return 0

    lax.fori_loop(0, chunks, chunk, 0)

    def owned(slot):
        request = jnp.int32(0)
        found = jnp.int32(0)
        for r in range(request_count):
            match = (owners_ref[r] == slot).astype(jnp.int32)
            request = request + r * match
            found = found + match
        start, end = request_span(lengths_ref, request, request_count)
        live = (found > 0) & (start <= last) & (end >= first)
        return request, jnp.maximum(end - last, 0), live

    def emit(out_ref, what):
        request, steps, live = what
        back = -steps.astype(F32)
        keep = jnp.where(live, 1.0, 0.0).astype(F32)
        for p, tile, at in each_tile(rate_ref):
            state = states[natural_rows(request * pole_count + p, tile, halves), :]
            out_ref[at] = state * (jnp.exp(rate_ref[at] * back) * keep)

    partner = jnp.where(lax.rem(i, 2) == 1, i - 1, i + 1)
    crossing = request_at(lengths_ref, last, request_count)
    for p, tile, at in each_tile(rate_ref):
        cross_ref[at] = states[natural_rows(crossing * pole_count + p, tile, halves), :]
    emit(near_ref, owned(partner))
    emit(own_ref, owned(i))
    for d in range(1, n // 2):
        emit(pair_ref.at[d - 1], owned(lax.rem(partner + 2 * d, n)))
        emit(mine_ref.at[d - 1], owned(lax.rem(i + 2 * d, n)))


def taps_kernel(bounds_ref, u_rows, decays, gains, skip_ref, y_rows, taps, lengths_ref):
    fill_lengths(bounds_ref, lengths_ref)
    halves = u_rows.shape[0]
    tok_dev = u_rows.shape[1] // SUBS
    pole_count = decays.shape[0] // (halves * SUBS)
    first = lax.axis_index("ctx") * tok_dev

    def half(h, _):
        skip = skip_ref[pl.ds(pl.multiple_of(h * SUBS, SUBS), SUBS), :]
        decay = [decays[state_rows(p, h, halves), :] for p in range(pole_count)]
        power = [gains[state_rows(p, h, halves), :] for p in range(pole_count)]
        for j in range(BLOCK):
            tap = total(list(power))
            taps[j * SUBS : (j + 1) * SUBS, :] = tap + skip if j == 0 else tap
            power = [x * a for x, a in zip(power, decay)]

        def request(r, start, lo, hi):
            head, begin, end, tail = block_parts(lo, hi)

            def alone(lo, hi):
                decay = [decays[state_rows(p, h, halves), :] for p in range(pole_count)]
                gain = [gains[state_rows(p, h, halves), :] for p in range(pole_count)]

                def single(t, state):
                    u = u_rows[h, token_rows(t), :]
                    state = tuple(s * a + u for s, a in zip(state, decay))
                    y_rows[h, token_rows(t), :] = total(
                        [s * g for s, g in zip(state, gain)] + [skip * u]
                    )
                    return state

                zero = jnp.zeros((SUBS, LANES), F32)
                lax.fori_loop(lo, hi, single, (zero,) * pole_count)

            @pl.when(head > lo)
            def _():
                alone(lo, head)

            @pl.when(hi > tail)
            def _():
                alone(tail, hi)

            tap = [taps[j * SUBS : (j + 1) * SUBS, :] for j in range(BLOCK)]

            def block(b, _):
                u = [u_rows[h, block_token(b, s), :] for s in range(BLOCK)]
                for s in range(BLOCK):
                    y_rows[h, block_token(b, s), :] = total(
                        [tap[j] * u[s - j] for j in range(s + 1)]
                    )
                return 0

            lax.fori_loop(begin, end, block, 0)

        each_request(lengths_ref, first, tok_dev, request)
        return 0

    lax.fori_loop(0, halves, half, 0)


def pool_kernel(mine_ref, pair_ref, *pooled_refs):
    for d, ref in enumerate(pooled_refs):
        for _, _, at in each_tile(ref):
            ref[at] = mine_ref[d, at[0], at[1]] + pair_ref[d, at[0], at[1]]


def finish_kernel(late, hops, bounds_ref, y_rows, saved, q_ref, decays, gains, rate_ref, *rest):
    hop_refs = rest[:hops]
    out_hbm, out_buf, w_rows, spread, fading, lengths_ref, out_sems = rest[hops + int(late) :]
    fill_lengths(bounds_ref, lengths_ref)
    tok_dev, channels = q_ref.shape
    halves = y_rows.shape[0]
    pole_count = rate_ref.shape[0]
    width, _ = half_span(channels)
    chunks = tok_dev // CHUNK
    first = lax.axis_index("ctx") * tok_dev
    before = request_before(lengths_ref, tok_dev, 1)
    reached = [
        (before >= 0) & (request_before(lengths_ref, tok_dev, hop) == before)
        for hop in range(1, max(hops, 2) + 1)
    ]
    _, end = request_span(lengths_ref, before, lengths_ref.shape[0])
    split = jnp.where(reached[1], jnp.minimum(end + 1 - first, tok_dev), 0)
    split = lax.div(split + (CHUNK - 1), jnp.int32(CHUNK))
    from_chunk, to_chunk = (0, split) if late else (split, chunks)

    def results(c, start):
        rows = (token_chunk(c), slice(None))
        chunk_copy(out_buf, rows, out_hbm, rows, out_sems.at[c], start)

    def incoming(at):
        state = jnp.zeros((SUBS, LANES), F32)
        for hop, ref in enumerate(hop_refs):
            moved = ref[at] * jnp.exp(rate_ref[at] * -float(hop * tok_dev)) if hop else ref[at]
            state = state + jnp.where(reached[hop], moved, 0.0)
        return state

    @pl.when(from_chunk < to_chunk)
    def _():
        to_states(rate_ref, spread, incoming)
        for p in range(pole_count):
            for h in range(halves):
                at = state_rows(p, h, halves)
                fading[h, state_rows(p, 0, 1), :] = spread[at, :] * gains[at, :] * decays[at, :]

    def gate(c):
        def block(b, _):
            rows = pl.ds(pl.multiple_of(c * CHUNK + b * PACKED, PACKED), PACKED)
            for h in range(halves):
                for j in range(width):
                    lanes = slice((h * SUBS + j) * LANES, (h * SUBS + j + 1) * LANES)
                    w = jnp.concatenate(
                        [
                            w_rows[h, tile_rows(b * (PACKED // SUBS) + part, j), :]
                            for part in range(PACKED // SUBS)
                        ],
                        axis=0,
                    )
                    out_buf[rows, lanes] = (q_ref[rows, lanes].astype(F32) * w).astype(jnp.bfloat16)
            return 0

        lax.fori_loop(0, CHUNK // PACKED, block, 0)

    def chunk(c, _):
        base = c * CHUNK

        def request(r, start, lo, hi):
            head, begin, end, tail = block_parts(lo, hi)

            def half(h, _):
                y = y_rows.at[h, pl.ds(pl.multiple_of(base * SUBS, CHUNK * SUBS), CHUNK * SUBS)]
                w = w_rows.at[h]

                @pl.when(start >= first)
                def _():
                    fading[h] = jnp.zeros(fading.shape[1:], F32)

                def keep(t, _):
                    w[token_rows(t), :] = y[token_rows(t), :]
                    return 0

                lax.fori_loop(lo, head, keep, 0)
                decay = [decays[state_rows(p, h, halves), :] for p in range(pole_count)]

                def opening(b):
                    state = []
                    for p in range(pole_count):
                        at = state_rows(p, h, halves)
                        local = saved[h, saved_rows(base // BLOCK + b, p, pole_count), :]
                        state.append(
                            local * (gains[at, :] * decays[at, :])
                            + fading[h, state_rows(p, 0, 1), :]
                        )
                    return state

                def block(b, _):
                    state = opening(b)
                    for p in range(pole_count):
                        at = state_rows(p, 0, 1)
                        power = decay[p]
                        for _ in range(BLOCK.bit_length() - 1):
                            power = power * power
                        fading[h, at, :] = fading[h, at, :] * power
                    for s in range(BLOCK):
                        rows = block_token(b, s)
                        w[rows, :] = y[rows, :] + total(list(state))
                        if s < BLOCK - 1:
                            state = [x * a for x, a in zip(state, decay)]
                    return 0

                lax.fori_loop(begin, end, block, 0)

                @pl.when(hi > tail)
                def _():
                    def single(t, state):
                        w[token_rows(t), :] = y[token_rows(t), :] + total(list(state))
                        return tuple(x * a for x, a in zip(state, decay))

                    lax.fori_loop(tail, hi, single, tuple(opening(end)))

                return 0

            lax.fori_loop(0, halves, half, 0)

        each_request(lengths_ref, first + base, CHUNK, request)
        gate(c)
        results(c, True)
        return 0

    def drain(c, _):
        results(c, False)
        return 0

    lax.fori_loop(from_chunk, to_chunk, chunk, 0)
    lax.fori_loop(from_chunk, to_chunk, drain, 0)


SMEM = pl.BlockSpec(memory_space=pltpu.SMEM)
VMEM = pl.BlockSpec(memory_space=pltpu.VMEM)
HBM = pl.BlockSpec(memory_space=pltpu.HBM)
DMA = pltpu.SemaphoreType.DMA


def in_hbm(x):
    return pltpu.with_memory_space_constraint(x, pltpu.HBM)


def call(kernel, name, out_shape, in_specs, out_specs, scratch=(), cost=(0, 0), aliases=None):
    return pl.pallas_call(
        kernel,
        out_shape=out_shape,
        in_specs=in_specs,
        out_specs=out_specs,
        scratch_shapes=list(scratch),
        compiler_params=pltpu.CompilerParams(vmem_limit_bytes=VMEM_BYTES),
        cost_estimate=pl.CostEstimate(flops=cost[0], bytes_accessed=cost[1], transcendentals=0),
        input_output_aliases=aliases or {},
        name=name,
    )


def rotate(block, distance):
    n = lax.axis_size("ctx")
    return lax.ppermute(block, "ctx", [(i, (i + distance) % n) for i in range(n)])


def trade(block):
    n = lax.axis_size("ctx")
    return lax.ppermute(block, "ctx", [(i, i ^ 1) for i in range(n)])


def shards(q_feat, k_feat, v_feat, pole_rate, residue, skip_gain, lengths, owners):
    tok_dev, channels = q_feat.shape
    pole_count = pole_rate.shape[0]
    request_count = lengths.shape[0]
    n = lax.axis_size("ctx")
    width, halves = half_span(channels)
    chunks = tok_dev // CHUNK
    longest = n * tok_dev // 2
    hops = -(-(longest - 1) // tok_dev)
    element = tok_dev * channels * pole_count
    token_bytes = tok_dev * channels
    one = jax.ShapeDtypeStruct((pole_count, channels), F32)
    all_rows = jax.ShapeDtypeStruct((halves, tok_dev * SUBS, LANES), F32)
    state_shape = jax.ShapeDtypeStruct((pole_count * halves * SUBS, LANES), F32)
    saved_shape = jax.ShapeDtypeStruct(
        (halves, tok_dev // BLOCK * pole_count * SUBS, LANES), F32
    )
    tokens = pltpu.VMEM((tok_dev, channels), jnp.bfloat16)

    def blocks(count):
        return jax.ShapeDtypeStruct((count, pole_count, channels), F32)

    cross, near_out, pair_out, own, mine, bounds, u_rows, decays, gains, saved = call(
        pieces_kernel,
        "pieces",
        [one, one, blocks(n // 2 - 1), one, blocks(n // 2 - 1)]
        + [jax.ShapeDtypeStruct((request_count, SUBS, LANES), F32), all_rows, state_shape, state_shape, saved_shape],
        [HBM] * 6,
        [VMEM] * 10,
        [
            tokens,
            tokens,
            pltpu.VMEM((pole_count, channels), F32),
            pltpu.VMEM((pole_count, channels), F32),
            pltpu.SMEM((request_count,), jnp.int32),
            pltpu.SMEM((request_count,), jnp.int32),
            pltpu.VMEM((request_count * pole_count * halves * SUBS, LANES), F32),
            DMA((2, tok_dev // LOAD)),
            DMA((4,)),
        ],
        (2 * element, 8 * token_bytes),
    )(*map(in_hbm, (lengths, owners, k_feat, v_feat, pole_rate, residue)))

    hop_in = [rotate(cross, 1)]
    pair_in = trade(pair_out)
    hop_in += [rotate(cross, hop) for hop in range(2, hops + 1)]

    skip_rows = skip_gain.reshape(-1, LANES)
    if skip_rows.shape[0] < SUBS:
        skip_rows = jnp.pad(skip_rows, ((0, SUBS - skip_rows.shape[0]), (0, 0)))
    y_rows = call(
        taps_kernel,
        "taps",
        all_rows,
        [VMEM] * 5,
        VMEM,
        [pltpu.VMEM((BLOCK * SUBS, LANES), F32), pltpu.SMEM((request_count,), jnp.int32)],
        (BLOCK * token_bytes, 8 * token_bytes),
    )(bounds, u_rows, decays, gains, skip_rows)

    near_out, y_rows = lax.optimization_barrier((near_out, y_rows))
    near_in = trade(near_out)
    pair_in, y_rows = lax.optimization_barrier((pair_in, y_rows))
    far_out = call(
        pool_kernel, "pool", [one] * (n // 2 - 1), [VMEM] * 2, [VMEM] * (n // 2 - 1)
    )(mine, pair_in)
    far_in = [rotate(block, 2 * d) for d, block in enumerate(far_out, 1)]

    mixed_shape = jax.ShapeDtypeStruct((tok_dev, channels), jnp.bfloat16)

    def finish(late, used, more):
        operands = [bounds, y_rows, saved, q_feat, decays, gains, pole_rate, *used]
        return call(
            functools.partial(finish_kernel, late, len(used)),
            "late" if late else "finish",
            mixed_shape,
            [VMEM] * (7 + len(used)) + [HBM] * len(more),
            HBM,
            [
                tokens,
                pltpu.VMEM((halves, CHUNK * SUBS, LANES), F32),
                pltpu.VMEM(state_shape.shape, F32),
                pltpu.VMEM((halves, pole_count * SUBS, LANES), F32),
                pltpu.SMEM((request_count,), jnp.int32),
                DMA((chunks,)),
            ],
            (2 * element, 8 * token_bytes),
            {len(operands): 0} if late else None,
        )(*operands, *more)

    mixed_out = finish(True, hop_in, [finish(False, hop_in[:1], [])])
    return mixed_out, sum(far_in, own + near_in)[None]


def solution(mesh):
    placed = (
        P(("groups", "ctx"), "chan"),
        P(("groups", "ctx"), "chan"),
        P(("groups", "ctx"), "chan"),
        P(None, "chan"),
        P(None, "chan"),
        P("chan"),
        P("groups"),
        P("groups"),
    )
    return jax.shard_map(
        shards,
        mesh=mesh,
        in_specs=placed,
        out_specs=(P(("groups", "ctx"), "chan"), P(("groups", "ctx"), None, "chan")),
        check_vma=False,
    )
```

profile of v0, /device:TPU:0, one launch (start us, length us, event | category | flops | bytes accessed | tf_op | source)
XLA Modules:
  0.0 31.8 jit_solution(9415945221838662651)
XLA Ops:
  0.6 0.0 copy-start.2
  0.6 8.7 %pieces.1 = (f32[16,2048]{1,0:T(8,128)S(1)}, f32[16,2048]{1,0:T(8,128)S(1)}, f32[1,16,2048]{2,1,0:T(8,128)S(1)}, f32[16,2048]{1,0:T(8,128)S(1)}, f32[1,16,2048]{...) custom-call(s32[4]{0:T(128)} %lengths_hbm.1, ...), custom_call_target="tpu_custom_call" | custom-call | flops 33554432 | bytes 8388608 | tf_op jit(solution)/shard_map/pieces/pallas_call | solution.py:550
  9.4 2.9 %collective-permute-start = (f32[1,16,2048]{2,1,0:T(8,128)S(1)}, f32[1,16,2048]{2,1,0:T(8,128)S(1)}, u32[]{:S(2)}, u32[]{:S(2)}) collective-permute-start(f32[1,16,2048]{2,1,0:T(8,128)S(1)} %get-tuple-element.17), channel_id=1, source_target_pairs={{0,4},{4,0},{8,12},{12,8},{1,5},{5,1},{9,13},{13,9},{2,6},{6,2},{1... | collective-permute-start | bytes 393224 | tf_op jit(solution)/shard_map/ppermute | solution.py:525
  12.3 0.1 collective-permute-start.1
  12.3 3.1 %collective-permute-start.2 = (f32[16,2048]{1,0:T(8,128)S(1)}, f32[16,2048]{1,0:T(8,128)S(1)}, u32[]{:S(2)}, u32[]{:S(2)}) collective-permute-start(f32[16,2048]{1,0:T(8,128)S(1)} %get-tuple-element.25), channel_id=1, source_target_pairs={{0,8},{4,12},{8,0},{12,4},{1,9},{5,13},{9,1},{13,5},{2,10},{6,14},... | collective-permute-start | bytes 393224 | tf_op jit(solution)/shard_map/ppermute | solution.py:520
  15.5 0.0 copy-done.2
  15.5 0.0 copy-start
  15.5 0.0 copy-start.1
  15.5 3.7 %taps.1.y_rows = f32[2,4096,128]{2,1,0:T(8,128)S(1)} custom-call(f32[4,8,128]{2,1,0:T(8,128)S(1)} %get-tuple-element.16.bounds_ref, f32[2,4096,128]{2,1,0:T(8,128)S(1)} %get-tuple-element.19.u_rows, f32[256,128]{1,0:T(8,128)S(1)} %get-tuple-element.20.decays, f32[256,128]{1,0:T(8,128)S(1)} %get-tuple-element.21.gains, f32[16,128]{1,0:T(8,128)S(1)} %bitcast.3), custom_call_target="tpu_custom_call" | custom-call | flops 16777216 | bytes 8388608 | tf_op jit(solution)/shard_map/taps/pallas_call | solution.py:578
  19.3 0.8 %collective-permute-start.3 = (f32[16,2048]{1,0:T(8,128)S(1)}, f32[16,2048]{1,0:T(8,128)S(1)}, u32[]{:S(2)}, u32[]{:S(2)}) collective-permute-start(f32[16,2048]{1,0:T(8,128)S(1)} %get-tuple-element.27), channel_id=1, source_target_pairs={{0,4},{4,0},{8,12},{12,8},{1,5},{5,1},{9,13},{13,9},{2,6},{6,2},{1... | collective-permute-start | bytes 393224 | tf_op jit(solution)/shard_map/ppermute | solution.py:525
  20.0 0.1 collective-permute-done.pair_ref
  20.1 2.3 %collective-permute-start.4 = (f32[16,2048]{1,0:T(8,128)S(1)}, f32[16,2048]{1,0:T(8,128)S(1)}, u32[]{:S(2)}, u32[]{:S(2)}) collective-permute-start(f32[16,2048]{1,0:T(8,128)S(1)} %pool.1), channel_id=1, source_target_pairs={{0,8},{4,12},{8,0},{12,4},{1,9},{5,13},{9,1},{13,5},{2,10},{6,14},... | collective-permute-start | bytes 393224 | tf_op jit(solution)/shard_map/ppermute | solution.py:520
  22.5 0.0 collective-permute-done.1.rest_0_
  22.5 0.0 copy-done
  22.5 0.0 copy-done.1
  22.5 8.4 %finish.1.rest_2_ = bf16[512,2048]{1,0:T(8,128)(2,1)} custom-call(f32[4,8,128]{2,1,0:T(8,128)S(1)} %get-tuple-element.16.bounds_ref, f32[2,4096,128]{2,1,0:T(8,128)S(1)} %taps.1.y_rows, f32[2,4096,128]{2,1,0:T(8,128)S(1)} %get-tuple-element.24.saved, bf16[512,2048]{1,0:T(8,128)(2,1)S(1)} %copy-done, f32[256,128]{1,0:T(8,128)S(1)} %get-tuple-element.20.decays, ...), custom_call_target="tpu_custom_call" | custom-call | flops 33554432 | bytes 8388608 | tf_op jit(solution)/shard_map/finish/pallas_call | solution.py:600
  30.9 0.0 collective-permute-done.2.rest_1_
  30.9 0.2 late.1
  31.1 0.0 collective-permute-done.3
  31.1 0.0 collective-permute-done.4
  31.1 0.7 %add_bitcast_fusion = f32[1,16,2048]{2,1,0:T(8,128)} fusion(f32[16,2048]{1,0:T(8,128)S(1)} %collective-permute-done.4, f32[16,2048]{1,0:T(8,128)S(1)} %get-tuple-element.26, f32[16,2048]{1,0:T(8,128)S(1)} %collective-permute-done.3), kind=kLoop, calls=%fused_computation | loop fusion | flops 65536 | bytes 524288 | tf_op jit(solution)/shard_map/broadcast_in_dim | solution.py:619
  (1 shorter events, 0.0 us)
Async XLA Ops:
  0.6 14.9 %copy-start.2 = (f32[2048]{0:T(1024)S(1)}, f32[2048]{0:T(1024)}, u32[]{:S(2)}) copy-start(f32[2048]{0:T(1024)} %param.13) | copy-start | bytes 24580
  9.4 10.8 %collective-permute-start = (f32[1,16,2048]{2,1,0:T(8,128)S(1)}, f32[1,16,2048]{2,1,0:T(8,128)S(1)}, u32[]{:S(2)}, u32[]{:S(2)}) collective-permute-start(f32[1,16,2048]{2,1,0:T(8,128)S(1)} %get-tuple-element.17), channel_id=1, source_target_pairs={{0,4},{4,0},{8,12},{12,8},{1,5},{5,1},{9,13},{13,9},{2,6},{6,2},{1... | collective-permute-start | bytes 393224 | tf_op jit(solution)/shard_map/ppermute | solution.py:525
  12.3 10.2 %collective-permute-start.1 = (f32[16,2048]{1,0:T(8,128)S(1)}, f32[16,2048]{1,0:T(8,128)S(1)}, u32[]{:S(2)}, u32[]{:S(2)}) collective-permute-start(f32[16,2048]{1,0:T(8,128)S(1)} %get-tuple-element.25), channel_id=1, source_target_pairs={{0,4},{4,8},{8,12},{12,0},{1,5},{5,9},{9,13},{13,1},{2,6},{6,10},{... | collective-permute-start | bytes 393224 | tf_op jit(solution)/shard_map/ppermute | solution.py:520
  12.3 18.5 %collective-permute-start.2 = (f32[16,2048]{1,0:T(8,128)S(1)}, f32[16,2048]{1,0:T(8,128)S(1)}, u32[]{:S(2)}, u32[]{:S(2)}) collective-permute-start(f32[16,2048]{1,0:T(8,128)S(1)} %get-tuple-element.25), channel_id=1, source_target_pairs={{0,8},{4,12},{8,0},{12,4},{1,9},{5,13},{9,1},{13,5},{2,10},{6,14},... | collective-permute-start | bytes 393224 | tf_op jit(solution)/shard_map/ppermute | solution.py:520
  15.5 7.0 %copy-start = (bf16[512,2048]{1,0:T(8,128)(2,1)S(1)}, bf16[512,2048]{1,0:T(8,128)(2,1)}, u32[]{:S(2)}) copy-start(bf16[512,2048]{1,0:T(8,128)(2,1)} %q_ref.3) | copy-start | bytes 6291460
  15.5 7.0 %copy-start.1 = (f32[16,2048]{1,0:T(8,128)S(1)}, f32[16,2048]{1,0:T(8,128)}, u32[]{:S(2)}) copy-start(f32[16,2048]{1,0:T(8,128)} %rate_ref.3) | copy-start | bytes 393220
  19.3 11.8 %collective-permute-start.3 = (f32[16,2048]{1,0:T(8,128)S(1)}, f32[16,2048]{1,0:T(8,128)S(1)}, u32[]{:S(2)}, u32[]{:S(2)}) collective-permute-start(f32[16,2048]{1,0:T(8,128)S(1)} %get-tuple-element.27), channel_id=1, source_target_pairs={{0,4},{4,0},{8,12},{12,8},{1,5},{5,1},{9,13},{13,9},{2,6},{6,2},{1... | collective-permute-start | bytes 393224 | tf_op jit(solution)/shard_map/ppermute | solution.py:525
  20.1 11.0 %collective-permute-start.4 = (f32[16,2048]{1,0:T(8,128)S(1)}, f32[16,2048]{1,0:T(8,128)S(1)}, u32[]{:S(2)}, u32[]{:S(2)}) collective-permute-start(f32[16,2048]{1,0:T(8,128)S(1)} %pool.1), channel_id=1, source_target_pairs={{0,8},{4,12},{8,0},{12,4},{1,9},{5,13},{9,1},{13,5},{2,10},{6,14},... | collective-permute-start | bytes 393224 | tf_op jit(solution)/shard_map/ppermute | solution.py:520
where the time goes:
time: 31.9 us; the launch traced here: 31.8 us
  Pallas kernels  21.1 us (66%)
  starting transfers between devices  9.22 us (29%)
  between operations  0.71 us (2%)
  other arithmetic  0.68 us (2%)
    pallas_call x1, Pallas kernels, shards(): call(pieces_kernel, 'pieces', [one, one, blocks(n // 2 - 1), one, blocks(...  8.72 us
    pallas_call x2, Pallas kernels, finish(): call(functools.partial(finish_kernel, late, len(used)), 'late' if late el...  8.59 us
    ppermute x3, starting transfers between devices, rotate(): lax.ppermute(block, 'ctx', [(i, (i + distance) % n) for i in range(n)])  5.53 us
    pallas_call x1, Pallas kernels, shards(): call(taps_kernel, 'taps', all_rows, [VMEM] * 5, VMEM, [pltpu.VMEM((BLOCK...  3.75 us
    ppermute x2, starting transfers between devices, trade(): return lax.ppermute(block, 'ctx', [(i, i ^ 1) for i in range(n)])  3.7 us
    broadcast_in_dim x1, other arithmetic, shards(): return (mixed_out, sum(far_in, own + near_in)[None])  0.68 us
  transfers between devices with their start and end apart: 5, of which 1 were waited for; matrix products, arithmetic and copies ran while one was open for 0% of the time, Pallas kernels for 39%

commit v1 on v0

--- a/solution.py
+++ b/solution.py
@@ -11,7 +11,7 @@
 SUBS = 8
 PACKED = 16
 LOAD = 256
-CHUNK = 128
+CHUNK = 256
 BLOCK = 16
 UNROLL = 8
 VMEM_BYTES = 28 * 1024 * 1024

time: 31.9 us -> 32.2 us (level); the launches traced: 31.8 us -> 31.7 us
    ppermute x2, starting transfers between devices: 3.7 us -> 4.68 us  [trade(): return lax.ppermute(block, 'ctx', [(i, i ^ 1) for i in range(n)])]
    ppermute x3, starting transfers between devices: 5.53 us -> 4.62 us  [rotate(): lax.ppermute(block, 'ctx', [(i, (i + distance) % n) for i in range(n)])]
  transfers between devices with their start and end apart: 5 -> 5, of which waited for: 1 -> 0; matrix products, arithmetic and copies ran while one was open for 0% -> 0% of each run, Pallas kernels for 39% -> 39%
where the time goes in v1:
time: 32.2 us; the launch traced here: 31.7 us
  Pallas kernels  20.9 us (65%)
  starting transfers between devices  9.3 us (29%)
  between operations  0.71 us (2%)
  other arithmetic  0.68 us (2%)
    pallas_call x1, Pallas kernels, shards(): call(pieces_kernel, 'pieces', [one, one, blocks(n // 2 - 1), one, blocks(...  8.72 us
    pallas_call x2, Pallas kernels, finish(): call(functools.partial(finish_kernel, late, len(used)), 'late' if late el...  8.47 us
    ppermute x2, starting transfers between devices, trade(): return lax.ppermute(block, 'ctx', [(i, i ^ 1) for i in range(n)])  4.68 us
    ppermute x3, starting transfers between devices, rotate(): lax.ppermute(block, 'ctx', [(i, (i + distance) % n) for i in range(n)])  4.62 us
    pallas_call x1, Pallas kernels, shards(): call(taps_kernel, 'taps', all_rows, [VMEM] * 5, VMEM, [pltpu.VMEM((BLOCK...  3.75 us
    broadcast_in_dim x1, other arithmetic, shards(): return (mixed_out, sum(far_in, own + near_in)[None])  0.68 us
  transfers between devices with their start and end apart: 5, of which 0 were waited for; matrix products, arithmetic and copies ran while one was open for 0% of the time, Pallas kernels for 39%

profile of v1, /device:TPU:0, one launch (start us, length us, event | category | flops | bytes accessed | tf_op | source)
XLA Modules:
  0.0 31.7 jit_solution(393644734193292813)
XLA Ops:
  0.6 0.0 copy-start.2
  0.6 8.7 %pieces.1 = (f32[16,2048]{1,0:T(8,128)S(1)}, f32[16,2048]{1,0:T(8,128)S(1)}, f32[1,16,2048]{2,1,0:T(8,128)S(1)}, f32[16,2048]{1,0:T(8,128)S(1)}, f32[1,16,2048]{...) custom-call(s32[4]{0:T(128)} %lengths_hbm.1, ...), custom_call_target="tpu_custom_call" | custom-call | flops 33554432 | bytes 8388608 | tf_op jit(solution)/shard_map/pieces/pallas_call | solution.py:550
  9.4 3.1 %collective-permute-start = (f32[1,16,2048]{2,1,0:T(8,128)S(1)}, f32[1,16,2048]{2,1,0:T(8,128)S(1)}, u32[]{:S(2)}, u32[]{:S(2)}) collective-permute-start(f32[1,16,2048]{2,1,0:T(8,128)S(1)} %get-tuple-element.17), channel_id=1, source_target_pairs={{0,4},{4,0},{8,12},{12,8},{1,5},{5,1},{9,13},{13,9},{2,6},{6,2},{1... | collective-permute-start | bytes 393224 | tf_op jit(solution)/shard_map/ppermute | solution.py:525
  12.5 0.1 collective-permute-start.1
  12.5 2.8 %collective-permute-start.2 = (f32[16,2048]{1,0:T(8,128)S(1)}, f32[16,2048]{1,0:T(8,128)S(1)}, u32[]{:S(2)}, u32[]{:S(2)}) collective-permute-start(f32[16,2048]{1,0:T(8,128)S(1)} %get-tuple-element.25), channel_id=1, source_target_pairs={{0,8},{4,12},{8,0},{12,4},{1,9},{5,13},{9,1},{13,5},{2,10},{6,14},... | collective-permute-start | bytes 393224 | tf_op jit(solution)/shard_map/ppermute | solution.py:520
  15.3 0.0 copy-done.2
  15.3 0.0 copy-start
  15.3 0.0 copy-start.1
  15.3 3.7 %taps.1.y_rows = f32[2,4096,128]{2,1,0:T(8,128)S(1)} custom-call(f32[4,8,128]{2,1,0:T(8,128)S(1)} %get-tuple-element.16.bounds_ref, f32[2,4096,128]{2,1,0:T(8,128)S(1)} %get-tuple-element.19.u_rows, f32[256,128]{1,0:T(8,128)S(1)} %get-tuple-element.20.decays, f32[256,128]{1,0:T(8,128)S(1)} %get-tuple-element.21.gains, f32[16,128]{1,0:T(8,128)S(1)} %bitcast.3), custom_call_target="tpu_custom_call" | custom-call | flops 16777216 | bytes 8388608 | tf_op jit(solution)/shard_map/taps/pallas_call | solution.py:578
  19.1 1.6 %collective-permute-start.3 = (f32[16,2048]{1,0:T(8,128)S(1)}, f32[16,2048]{1,0:T(8,128)S(1)}, u32[]{:S(2)}, u32[]{:S(2)}) collective-permute-start(f32[16,2048]{1,0:T(8,128)S(1)} %get-tuple-element.27), channel_id=1, source_target_pairs={{0,4},{4,0},{8,12},{12,8},{1,5},{5,1},{9,13},{13,9},{2,6},{6,2},{1... | collective-permute-start | bytes 393224 | tf_op jit(solution)/shard_map/ppermute | solution.py:525
  20.7 0.0 collective-permute-done.pair_ref
  20.7 1.8 %collective-permute-start.4 = (f32[16,2048]{1,0:T(8,128)S(1)}, f32[16,2048]{1,0:T(8,128)S(1)}, u32[]{:S(2)}, u32[]{:S(2)}) collective-permute-start(f32[16,2048]{1,0:T(8,128)S(1)} %pool.1), channel_id=1, source_target_pairs={{0,8},{4,12},{8,0},{12,4},{1,9},{5,13},{9,1},{13,5},{2,10},{6,14},... | collective-permute-start | bytes 393224 | tf_op jit(solution)/shard_map/ppermute | solution.py:520
  22.5 0.0 collective-permute-done.1.rest_0_
  22.5 0.0 copy-done
  22.5 0.0 copy-done.1
  22.5 8.3 %finish.1.rest_2_ = bf16[512,2048]{1,0:T(8,128)(2,1)} custom-call(f32[4,8,128]{2,1,0:T(8,128)S(1)} %get-tuple-element.16.bounds_ref, f32[2,4096,128]{2,1,0:T(8,128)S(1)} %taps.1.y_rows, f32[2,4096,128]{2,1,0:T(8,128)S(1)} %get-tuple-element.24.saved, bf16[512,2048]{1,0:T(8,128)(2,1)S(1)} %copy-done, f32[256,128]{1,0:T(8,128)S(1)} %get-tuple-element.20.decays, ...), custom_call_target="tpu_custom_call" | custom-call | flops 33554432 | bytes 8388608 | tf_op jit(solution)/shard_map/finish/pallas_call | solution.py:600
  30.8 0.0 collective-permute-done.2.rest_1_
  30.8 0.2 late.1
  31.0 0.0 collective-permute-done.3
  31.0 0.0 collective-permute-done.4
  31.0 0.7 %add_bitcast_fusion = f32[1,16,2048]{2,1,0:T(8,128)} fusion(f32[16,2048]{1,0:T(8,128)S(1)} %collective-permute-done.4, f32[16,2048]{1,0:T(8,128)S(1)} %get-tuple-element.26, f32[16,2048]{1,0:T(8,128)S(1)} %collective-permute-done.3), kind=kLoop, calls=%fused_computation | loop fusion | flops 65536 | bytes 524288 | tf_op jit(solution)/shard_map/broadcast_in_dim | solution.py:619
  (1 shorter events, 0.0 us)
Async XLA Ops:
  0.6 14.7 %copy-start.2 = (f32[2048]{0:T(1024)S(1)}, f32[2048]{0:T(1024)}, u32[]{:S(2)}) copy-start(f32[2048]{0:T(1024)} %param.13) | copy-start | bytes 24580
  9.4 11.3 %collective-permute-start = (f32[1,16,2048]{2,1,0:T(8,128)S(1)}, f32[1,16,2048]{2,1,0:T(8,128)S(1)}, u32[]{:S(2)}, u32[]{:S(2)}) collective-permute-start(f32[1,16,2048]{2,1,0:T(8,128)S(1)} %get-tuple-element.17), channel_id=1, source_target_pairs={{0,4},{4,0},{8,12},{12,8},{1,5},{5,1},{9,13},{13,9},{2,6},{6,2},{1... | collective-permute-start | bytes 393224 | tf_op jit(solution)/shard_map/ppermute | solution.py:525
  12.5 10.0 %collective-permute-start.1 = (f32[16,2048]{1,0:T(8,128)S(1)}, f32[16,2048]{1,0:T(8,128)S(1)}, u32[]{:S(2)}, u32[]{:S(2)}) collective-permute-start(f32[16,2048]{1,0:T(8,128)S(1)} %get-tuple-element.25), channel_id=1, source_target_pairs={{0,4},{4,8},{8,12},{12,0},{1,5},{5,9},{9,13},{13,1},{2,6},{6,10},{... | collective-permute-start | bytes 393224 | tf_op jit(solution)/shard_map/ppermute | solution.py:520
  12.5 18.2 %collective-permute-start.2 = (f32[16,2048]{1,0:T(8,128)S(1)}, f32[16,2048]{1,0:T(8,128)S(1)}, u32[]{:S(2)}, u32[]{:S(2)}) collective-permute-start(f32[16,2048]{1,0:T(8,128)S(1)} %get-tuple-element.25), channel_id=1, source_target_pairs={{0,8},{4,12},{8,0},{12,4},{1,9},{5,13},{9,1},{13,5},{2,10},{6,14},... | collective-permute-start | bytes 393224 | tf_op jit(solution)/shard_map/ppermute | solution.py:520
  15.3 7.1 %copy-start = (bf16[512,2048]{1,0:T(8,128)(2,1)S(1)}, bf16[512,2048]{1,0:T(8,128)(2,1)}, u32[]{:S(2)}) copy-start(bf16[512,2048]{1,0:T(8,128)(2,1)} %q_ref.3) | copy-start | bytes 6291460
  15.3 7.1 %copy-start.1 = (f32[16,2048]{1,0:T(8,128)S(1)}, f32[16,2048]{1,0:T(8,128)}, u32[]{:S(2)}) copy-start(f32[16,2048]{1,0:T(8,128)} %rate_ref.3) | copy-start | bytes 393220
  19.1 11.9 %collective-permute-start.3 = (f32[16,2048]{1,0:T(8,128)S(1)}, f32[16,2048]{1,0:T(8,128)S(1)}, u32[]{:S(2)}, u32[]{:S(2)}) collective-permute-start(f32[16,2048]{1,0:T(8,128)S(1)} %get-tuple-element.27), channel_id=1, source_target_pairs={{0,4},{4,0},{8,12},{12,8},{1,5},{5,1},{9,13},{13,9},{2,6},{6,2},{1... | collective-permute-start | bytes 393224 | tf_op jit(solution)/shard_map/ppermute | solution.py:525
  20.7 10.3 %collective-permute-start.4 = (f32[16,2048]{1,0:T(8,128)S(1)}, f32[16,2048]{1,0:T(8,128)S(1)}, u32[]{:S(2)}, u32[]{:S(2)}) collective-permute-start(f32[16,2048]{1,0:T(8,128)S(1)} %pool.1), channel_id=1, source_target_pairs={{0,8},{4,12},{8,0},{12,4},{1,9},{5,13},{9,1},{13,5},{2,10},{6,14},... | collective-permute-start | bytes 393224 | tf_op jit(solution)/shard_map/ppermute | solution.py:520
